TPU v7x, 32 devices: a whole 2x2x4 slice. The times are simulated.
32 devices in a mesh: parts: 2 (over y), span: 4 (over x, core), seq: 4 (over z).
Axes of the slice: x: 2, y: 2, z: 4, core: 2. Of those that a mesh axis runs over, the one named last changes fastest.
Arguments:
- q_in: bfloat16 [8, 1024, 4096], P(('parts', 'span'), 'seq'), parts along dimension 0, may hold values from -9 to 9
- k_in: bfloat16 [8, 1024, 4096], P(('parts', 'span'), 'seq'), parts along dimension 0, may hold values from -9 to 9
- v_in: bfloat16 [8, 1024, 4096], P(('parts', 'span'), 'seq'), parts along dimension 0, may hold values from -18 to 18
- timesteps: int32 [8], P('parts'), parts along dimension 0, may hold values from 0 to 31
- gate_table: float32 [32, 4096], replicated, may hold values from 0.1 to 1.9
Outputs:
- gated_out: bfloat16 [8, 1024, 4096], P(('parts', 'span'), 'seq'), parts along dimension 0
There are 2 independent parts, one for each index of `parts`. A program takes and returns all parts, laid end to end along the dimension named above; an argument that names none is the same for every part. Nothing has to cross between parts.
All inputs are finite; a program needn't handle non-finite values.
Results may differ from a plain program's by a relative error of at most 0.0053.
Values may be sent and summed in bfloat16 or wider, within the bound.
A program may use at most 128 MiB of HBM per device.

v0:
```python
import math
import jax
import jax.numpy as jnp
from jax import lax
from jax.sharding import PartitionSpec as P

HD = 128
masked_score = -1e30


def local(q_in, k_in, v_in, timesteps, gate_table):
    head_rows, key_rows, value_rows = (
        lax.all_to_all(q_in[0], "seq", split_axis=1, concat_axis=0, tiled=True),
        lax.all_to_all(k_in[0], "seq", split_axis=1, concat_axis=0, tiled=True),
        lax.all_to_all(v_in[0], "seq", split_axis=1, concat_axis=0, tiled=True),
    )
    length = head_rows.shape[0]
    columns = head_rows.shape[1]
    heads = columns // HD
    scale = HD ** (-0.5)
    span_id = lax.axis_index("span")
    limit = (span_id + 1) * length
    query_three = head_rows.reshape(length, heads, HD)
    init = (
        jnp.full((heads, length), masked_score, jnp.float32),
        jnp.zeros((heads, length), jnp.float32),
        jnp.zeros((length, heads, HD), jnp.float32),
    )
    key_piece = lax.all_gather(key_rows, "span", axis=0, tiled=True)
    value_piece = lax.all_gather(value_rows, "span", axis=0, tiled=True)
    count = key_piece.shape[0]
    block = math.gcd(count, 512)

    def one_block(index, state):
        top, total, accum = state
        offset = index * block
        key_block = lax.dynamic_slice_in_dim(key_piece, offset, block, 0).reshape(block, heads, HD)
        value_block = lax.dynamic_slice_in_dim(value_piece, offset, block, 0).reshape(
            block, heads, HD
        )
        scores = (
            jnp.einsum("qhd,khd->hqk", query_three, key_block, preferred_element_type=jnp.float32)
            * scale
        )
        keep = offset + jnp.arange(block) < limit
        scores = jnp.where(keep[None, None, :], scores, masked_score)
        new_top = jnp.maximum(top, jnp.max(scores, axis=-1))
        expo = jnp.where(keep[None, None, :], jnp.exp(scores - new_top[:, :, None]), 0.0)
        shrink = jnp.exp(top - new_top)
        total = total * shrink + jnp.sum(expo, axis=-1)
        mixed = jnp.einsum(
            "hqk,khd->qhd",
            expo.astype(jnp.bfloat16),
            value_block,
            preferred_element_type=jnp.float32,
        )
        accum = accum * shrink.T[:, :, None] + mixed
        return (new_top, total, accum)

    def run_blocks(state):
        return lax.fori_loop(0, count // block, one_block, state)

    def keep_state(state):
        return state

    top, total, accum = lax.cond(jnp.int32(0) < limit, run_blocks, keep_state, init)
    attn = (accum / total.T[:, :, None]).reshape(length, columns).astype(jnp.bfloat16)
    token_rows = lax.all_to_all(attn, "seq", split_axis=0, concat_axis=1, tiled=True)
    steps_count = gate_table.shape[0]
    span_step = lax.dynamic_index_in_dim(timesteps, span_id, 0, keepdims=False)
    picked = (jnp.arange(steps_count) == span_step).astype(jnp.float32)
    gate = jnp.dot(picked, gate_table, precision=lax.Precision.HIGHEST)
    return (token_rows.astype(jnp.float32) * gate[None, :]).astype(jnp.bfloat16)[None]


def solution(mesh):
    in_specs = (
        P(("parts", "span"), "seq", None),
        P(("parts", "span"), "seq", None),
        P(("parts", "span"), "seq", None),
        P("parts"),
        P(),
    )
    out_specs = P(("parts", "span"), "seq", None)
    return jax.shard_map(local, mesh=mesh, in_specs=in_specs, out_specs=out_specs, check_vma=False)
```

profile of v0, /device:TPU:0, one launch (start us, length us, event | category | flops | bytes accessed | tf_op | source)
XLA Modules:
  0.0 533.7 jit_solution(13859830746761117424)
XLA Ops:
  6.5 4.1 copy.30
  10.7 54.5 %all_to_all.64 = bf16[256,4,1024]{0,2,1:T(8,128)(2,1)S(1)} all-to-all(bf16[256,4,1024]{0,2,1:T(8,128)(2,1)} %bitcast.80), channel_id=1, replica_groups=mesh['parts'=2,'span'=4,'seq'=4] {'seq'}, dimensions={1} | all-to-all | bytes 4194304 | tf_op jit(solution)/shard_map/all_to_all | solution.py:14
  65.2 2.5 copy.31
  67.7 4.1 copy.32
  71.8 51.0 %all_to_all.65 = bf16[256,4,1024]{0,2,1:T(8,128)(2,1)S(1)} all-to-all(bf16[256,4,1024]{0,2,1:T(8,128)(2,1)} %bitcast.81), channel_id=1, replica_groups=mesh['parts'=2,'span'=4,'seq'=4] {'seq'}, dimensions={1} | all-to-all | bytes 4194304 | tf_op jit(solution)/shard_map/all_to_all | solution.py:15
  122.8 2.4 copy.33
  125.2 4.1 copy.29
  129.3 3.6 all-to-all-start
  132.9 47.3 %all-to-all-done = bf16[256,4,1024]{0,2,1:T(8,128)(2,1)S(1)} async-done(((bf16[256,4,1024]{0,2,1:T(8,128)(2,1)}), bf16[256,4,1024]{0,2,1:T(8,128)(2,1)S(1)}, u32[]{:S(2)}, u32[]{:S(2)}) %all-to-all-start) | async-done | bytes 2097184 | tf_op jit(solution)/shard_map/all_to_all | solution.py:13
  180.2 5.0 all-gather.5.cloned.1.call-done
  185.2 271.6 %conditional.1 = (f32[8,1024]{1,0:T(8,128)}, f32[1024,8,128]{0,2,1:T(8,128)}) conditional(s32[]{:T(128)} %convert_element_type.44, () %tuple.27, (bf16[4,256,1024]{1,2,0:T(8,128)(2,1)S(1)}, s32[]{:T(128)}, bf16[4096,1024]{1,0:T(8,128)(2,1)}, bf16[4096,1024]{1,0:T(8,128)(2,1)}) %tuple.65), branch_computations={%region_0.0_spmd, %region_1.6_spmd} | conditional | flops 2205205504 | bytes 151521616 | solution.py:66
  185.2 2.4 copy.34
  187.6 2.2 copy.45
  189.8 1.7 copy.28
  191.5 265.3 %while.17 = (s32[]{:T(128)}, f32[8,1024]{1,0:T(8,128)S(1)}, f32[8,1024]{1,0:T(8,128)}, f32[1024,8,128]{0,2,1:T(8,128)}, s32[]{:T(128)}, /*index=5*/bf16[4096,102...) while((s32[]{:T(128)}, f32[8,1024]{1,0:T(8,128)S(1)}, ...), condition=%wide.region_5.5_spmd.clone, body=%wide.region_2.4_spmd.clone.sunk | while | flops 2205205504 | bytes 138938576 | solution.py:61
  191.5 2.7 constant_dynamic-slice_fusion.3
  194.2 1.5 copy.48
  195.7 9.4 %bitcast_reduce_fusion.2 = (f32[8,1024]{1,0:T(8,128)S(1)}, f32[8,512,1024]{2,1,0:T(8,128)}) fusion(pred[512]{0:T(512)(128)(4,1)S(1)} %add_compare_fusion.2, bf16[512,8,128]{0,2,1:T(8,128)(2,1)S(1)} %bitcast.72, bf16[1024,8,128]{2,0,1:T(8,128)(2,1)} %get-tuple-element.338), kind=kOutput, calls=%fused_computation.1.clone.1 | convolution fusion | flops 1086316544 | bytes 19956224 | tf_op jit(solution)/shard_map/cond/branch_1_fun/while/body/eval_jaxpr/qhd,khd->hqk/dot_general | solution.py:42
  205.6 10.9 %bitcast_add_fusion.2 = f32[1024,8,128]{0,2,1:T(8,128)} fusion(f32[1024,8,128]{0,2,1:T(8,128)} %get-tuple-element.323, bf16[512,8,128]{0,2,1:T(8,128)(2,1)S(1)} %bitcast.73, f32[8,512,1024]{2,1,0:T(8,128)} %get-tuple-element.305, f32[8,1024]{1,0:T(8,128)S(1)} %get-tuple-element.333, pred[512]{0:T(512)(128)(4,1)S(1)} %add_compare_fusion.2, ...), kind=kOutput, calls=%fused_computation.10.clone.1 | convolution fusion | flops 1097859072 | bytes 26280448 | tf_op jit(solution)/shard_map/cond/branch_1_fun/while/body/eval_jaxpr/hqk,khd->qhd/dot_general | solution.py:51
  217.7 4.6 fusion.37
  222.9 2.7 constant_dynamic-slice_fusion.3
  225.6 1.5 copy.48
  227.1 9.4 %bitcast_reduce_fusion.2 = (f32[8,1024]{1,0:T(8,128)S(1)}, f32[8,512,1024]{2,1,0:T(8,128)}) fusion(pred[512]{0:T(512)(128)(4,1)S(1)} %add_compare_fusion.2, bf16[512,8,128]{0,2,1:T(8,128)(2,1)S(1)} %bitcast.72, bf16[1024,8,128]{2,0,1:T(8,128)(2,1)} %get-tuple-element.338), kind=kOutput, calls=%fused_computation.1.clone.1 | convolution fusion | flops 1086316544 | bytes 19956224 | tf_op jit(solution)/shard_map/cond/branch_1_fun/while/body/eval_jaxpr/qhd,khd->hqk/dot_general | solution.py:42
  237.1 12.1 %bitcast_add_fusion.2 = f32[1024,8,128]{0,2,1:T(8,128)} fusion(f32[1024,8,128]{0,2,1:T(8,128)} %get-tuple-element.323, bf16[512,8,128]{0,2,1:T(8,128)(2,1)S(1)} %bitcast.73, f32[8,512,1024]{2,1,0:T(8,128)} %get-tuple-element.305, f32[8,1024]{1,0:T(8,128)S(1)} %get-tuple-element.333, pred[512]{0:T(512)(128)(4,1)S(1)} %add_compare_fusion.2, ...), kind=kOutput, calls=%fused_computation.10.clone.1 | convolution fusion | flops 1097859072 | bytes 26280448 | tf_op jit(solution)/shard_map/cond/branch_1_fun/while/body/eval_jaxpr/hqk,khd->qhd/dot_general | solution.py:51
  250.3 4.6 fusion.37
  256.3 2.7 constant_dynamic-slice_fusion.3
  259.0 1.5 copy.48
  260.5 9.4 %bitcast_reduce_fusion.2 = (f32[8,1024]{1,0:T(8,128)S(1)}, f32[8,512,1024]{2,1,0:T(8,128)}) fusion(pred[512]{0:T(512)(128)(4,1)S(1)} %add_compare_fusion.2, bf16[512,8,128]{0,2,1:T(8,128)(2,1)S(1)} %bitcast.72, bf16[1024,8,128]{2,0,1:T(8,128)(2,1)} %get-tuple-element.338), kind=kOutput, calls=%fused_computation.1.clone.1 | convolution fusion | flops 1086316544 | bytes 19956224 | tf_op jit(solution)/shard_map/cond/branch_1_fun/while/body/eval_jaxpr/qhd,khd->hqk/dot_general | solution.py:42
  270.5 12.1 %bitcast_add_fusion.2 = f32[1024,8,128]{0,2,1:T(8,128)} fusion(f32[1024,8,128]{0,2,1:T(8,128)} %get-tuple-element.323, bf16[512,8,128]{0,2,1:T(8,128)(2,1)S(1)} %bitcast.73, f32[8,512,1024]{2,1,0:T(8,128)} %get-tuple-element.305, f32[8,1024]{1,0:T(8,128)S(1)} %get-tuple-element.333, pred[512]{0:T(512)(128)(4,1)S(1)} %add_compare_fusion.2, ...), kind=kOutput, calls=%fused_computation.10.clone.1 | convolution fusion | flops 1097859072 | bytes 26280448 | tf_op jit(solution)/shard_map/cond/branch_1_fun/while/body/eval_jaxpr/hqk,khd->qhd/dot_general | solution.py:51
  283.7 4.6 fusion.37
  288.4 1.4 fusion.38
  289.8 2.7 constant_dynamic-slice_fusion.3
  292.4 1.5 copy.48
  293.9 9.4 %bitcast_reduce_fusion.2 = (f32[8,1024]{1,0:T(8,128)S(1)}, f32[8,512,1024]{2,1,0:T(8,128)}) fusion(pred[512]{0:T(512)(128)(4,1)S(1)} %add_compare_fusion.2, bf16[512,8,128]{0,2,1:T(8,128)(2,1)S(1)} %bitcast.72, bf16[1024,8,128]{2,0,1:T(8,128)(2,1)} %get-tuple-element.338), kind=kOutput, calls=%fused_computation.1.clone.1 | convolution fusion | flops 1086316544 | bytes 19956224 | tf_op jit(solution)/shard_map/cond/branch_1_fun/while/body/eval_jaxpr/qhd,khd->hqk/dot_general | solution.py:42
  303.9 12.1 %bitcast_add_fusion.2 = f32[1024,8,128]{0,2,1:T(8,128)} fusion(f32[1024,8,128]{0,2,1:T(8,128)} %get-tuple-element.323, bf16[512,8,128]{0,2,1:T(8,128)(2,1)S(1)} %bitcast.73, f32[8,512,1024]{2,1,0:T(8,128)} %get-tuple-element.305, f32[8,1024]{1,0:T(8,128)S(1)} %get-tuple-element.333, pred[512]{0:T(512)(128)(4,1)S(1)} %add_compare_fusion.2, ...), kind=kOutput, calls=%fused_computation.10.clone.1 | convolution fusion | flops 1097859072 | bytes 26280448 | tf_op jit(solution)/shard_map/cond/branch_1_fun/while/body/eval_jaxpr/hqk,khd->qhd/dot_general | solution.py:51
  317.1 4.6 fusion.37
  321.8 1.4 fusion.38
  323.2 2.7 constant_dynamic-slice_fusion.3
  325.8 1.5 copy.48
  327.4 9.4 %bitcast_reduce_fusion.2 = (f32[8,1024]{1,0:T(8,128)S(1)}, f32[8,512,1024]{2,1,0:T(8,128)}) fusion(pred[512]{0:T(512)(128)(4,1)S(1)} %add_compare_fusion.2, bf16[512,8,128]{0,2,1:T(8,128)(2,1)S(1)} %bitcast.72, bf16[1024,8,128]{2,0,1:T(8,128)(2,1)} %get-tuple-element.338), kind=kOutput, calls=%fused_computation.1.clone.1 | convolution fusion | flops 1086316544 | bytes 19956224 | tf_op jit(solution)/shard_map/cond/branch_1_fun/while/body/eval_jaxpr/qhd,khd->hqk/dot_general | solution.py:42
  337.3 12.1 %bitcast_add_fusion.2 = f32[1024,8,128]{0,2,1:T(8,128)} fusion(f32[1024,8,128]{0,2,1:T(8,128)} %get-tuple-element.323, bf16[512,8,128]{0,2,1:T(8,128)(2,1)S(1)} %bitcast.73, f32[8,512,1024]{2,1,0:T(8,128)} %get-tuple-element.305, f32[8,1024]{1,0:T(8,128)S(1)} %get-tuple-element.333, pred[512]{0:T(512)(128)(4,1)S(1)} %add_compare_fusion.2, ...), kind=kOutput, calls=%fused_computation.10.clone.1 | convolution fusion | flops 1097859072 | bytes 26280448 | tf_op jit(solution)/shard_map/cond/branch_1_fun/while/body/eval_jaxpr/hqk,khd->qhd/dot_general | solution.py:51
  350.5 4.6 fusion.37
  356.6 2.7 constant_dynamic-slice_fusion.3
  359.3 1.5 copy.48
  360.8 9.4 %bitcast_reduce_fusion.2 = (f32[8,1024]{1,0:T(8,128)S(1)}, f32[8,512,1024]{2,1,0:T(8,128)}) fusion(pred[512]{0:T(512)(128)(4,1)S(1)} %add_compare_fusion.2, bf16[512,8,128]{0,2,1:T(8,128)(2,1)S(1)} %bitcast.72, bf16[1024,8,128]{2,0,1:T(8,128)(2,1)} %get-tuple-element.338), kind=kOutput, calls=%fused_computation.1.clone.1 | convolution fusion | flops 1086316544 | bytes 19956224 | tf_op jit(solution)/shard_map/cond/branch_1_fun/while/body/eval_jaxpr/qhd,khd->hqk/dot_general | solution.py:42
  370.7 12.1 %bitcast_add_fusion.2 = f32[1024,8,128]{0,2,1:T(8,128)} fusion(f32[1024,8,128]{0,2,1:T(8,128)} %get-tuple-element.323, bf16[512,8,128]{0,2,1:T(8,128)(2,1)S(1)} %bitcast.73, f32[8,512,1024]{2,1,0:T(8,128)} %get-tuple-element.305, f32[8,1024]{1,0:T(8,128)S(1)} %get-tuple-element.333, pred[512]{0:T(512)(128)(4,1)S(1)} %add_compare_fusion.2, ...), kind=kOutput, calls=%fused_computation.10.clone.1 | convolution fusion | flops 1097859072 | bytes 26280448 | tf_op jit(solution)/shard_map/cond/branch_1_fun/while/body/eval_jaxpr/hqk,khd->qhd/dot_general | solution.py:51
  383.9 4.6 fusion.37
  390.0 2.7 constant_dynamic-slice_fusion.3
  392.7 1.5 copy.48
  394.2 9.4 %bitcast_reduce_fusion.2 = (f32[8,1024]{1,0:T(8,128)S(1)}, f32[8,512,1024]{2,1,0:T(8,128)}) fusion(pred[512]{0:T(512)(128)(4,1)S(1)} %add_compare_fusion.2, bf16[512,8,128]{0,2,1:T(8,128)(2,1)S(1)} %bitcast.72, bf16[1024,8,128]{2,0,1:T(8,128)(2,1)} %get-tuple-element.338), kind=kOutput, calls=%fused_computation.1.clone.1 | convolution fusion | flops 1086316544 | bytes 19956224 | tf_op jit(solution)/shard_map/cond/branch_1_fun/while/body/eval_jaxpr/qhd,khd->hqk/dot_general | solution.py:42
  404.1 12.1 %bitcast_add_fusion.2 = f32[1024,8,128]{0,2,1:T(8,128)} fusion(f32[1024,8,128]{0,2,1:T(8,128)} %get-tuple-element.323, bf16[512,8,128]{0,2,1:T(8,128)(2,1)S(1)} %bitcast.73, f32[8,512,1024]{2,1,0:T(8,128)} %get-tuple-element.305, f32[8,1024]{1,0:T(8,128)S(1)} %get-tuple-element.333, pred[512]{0:T(512)(128)(4,1)S(1)} %add_compare_fusion.2, ...), kind=kOutput, calls=%fused_computation.10.clone.1 | convolution fusion | flops 1097859072 | bytes 26280448 | tf_op jit(solution)/shard_map/cond/branch_1_fun/while/body/eval_jaxpr/hqk,khd->qhd/dot_general | solution.py:51
  417.4 4.6 fusion.37
  423.4 2.7 constant_dynamic-slice_fusion.3
  426.1 1.5 copy.48
  427.6 9.4 %bitcast_reduce_fusion.2 = (f32[8,1024]{1,0:T(8,128)S(1)}, f32[8,512,1024]{2,1,0:T(8,128)}) fusion(pred[512]{0:T(512)(128)(4,1)S(1)} %add_compare_fusion.2, bf16[512,8,128]{0,2,1:T(8,128)(2,1)S(1)} %bitcast.72, bf16[1024,8,128]{2,0,1:T(8,128)(2,1)} %get-tuple-element.338), kind=kOutput, calls=%fused_computation.1.clone.1 | convolution fusion | flops 1086316544 | bytes 19956224 | tf_op jit(solution)/shard_map/cond/branch_1_fun/while/body/eval_jaxpr/qhd,khd->hqk/dot_general | solution.py:42
  437.5 12.1 %bitcast_add_fusion.2 = f32[1024,8,128]{0,2,1:T(8,128)} fusion(f32[1024,8,128]{0,2,1:T(8,128)} %get-tuple-element.323, bf16[512,8,128]{0,2,1:T(8,128)(2,1)S(1)} %bitcast.73, f32[8,512,1024]{2,1,0:T(8,128)} %get-tuple-element.305, f32[8,1024]{1,0:T(8,128)S(1)} %get-tuple-element.333, pred[512]{0:T(512)(128)(4,1)S(1)} %add_compare_fusion.2, ...), kind=kOutput, calls=%fused_computation.10.clone.1 | convolution fusion | flops 1097859072 | bytes 26280448 | tf_op jit(solution)/shard_map/cond/branch_1_fun/while/body/eval_jaxpr/hqk,khd->qhd/dot_general | solution.py:51
  450.8 4.6 fusion.37
  456.8 2.8 divide_convert_fusion
  459.6 2.8 reshape.90
  462.4 4.3 copy.42
  466.7 4.6 all-to-all-start.3
  472.8 47.3 %all-to-all-done.3 = bf16[4,256,1024]{2,1,0:T(8,128)(2,1)} async-done(((bf16[4,256,1024]{2,1,0:T(8,128)(2,1)}), bf16[4,256,1024]{2,1,0:T(8,128)(2,1)}, u32[]{:S(2)}, u32[]{:S(2)}) %all-to-all-start.3) | async-done | bytes 2097184 | tf_op jit(solution)/shard_map/all_to_all | solution.py:68
  520.1 2.8 copy.38
  524.0 2.9 copy.39
  (70 shorter events, 24.3 us)
Async XLA Ops:
  6.5 465.3 %copy-start = (f32[32,4096]{1,0:T(8,128)S(1)}, f32[32,4096]{1,0:T(8,128)}, u32[]{:S(2)}) copy-start(f32[32,4096]{1,0:T(8,128)} %param.13) | copy-start | bytes 1572868
  6.5 173.7 %all-gather.3.cloned.1.call-start = ((), (), s32[]{:S(2)}) async-start(), calls=%async_computation.4 | async-start | bytes 10485760 | tf_op jit(solution)/shard_map/all_gather | solution.py:29
  67.7 117.5 %all-gather.5.cloned.1.call-start = ((), (), s32[]{:S(2)}) async-start(), calls=%async_computation.5 | async-start | bytes 10485760 | tf_op jit(solution)/shard_map/all_gather | solution.py:30
  129.3 50.9 %all-to-all-start = ((bf16[256,4,1024]{0,2,1:T(8,128)(2,1)}), bf16[256,4,1024]{0,2,1:T(8,128)(2,1)S(1)}, u32[]{:S(2)}, u32[]{:S(2)}) async-start(bf16[256,4,1024]{0,2,1:T(8,128)(2,1)} %bitcast.78), calls=%async_computation | async-start | bytes 4194304 | tf_op jit(solution)/shard_map/all_to_all | solution.py:13
  205.6 12.1 %copy-start.1 = (f32[8,512,1024]{2,1,0:T(8,128)S(1)}, f32[8,512,1024]{2,1,0:T(8,128)}, u32[]{:S(2)}) copy-start(f32[8,512,1024]{2,1,0:T(8,128)} %get-tuple-element.305) | copy-start | bytes 50331652 | tf_op jit(solution)/shard_map/cond/branch_1_fun/while
  237.1 13.3 %copy-start.1 = (f32[8,512,1024]{2,1,0:T(8,128)S(1)}, f32[8,512,1024]{2,1,0:T(8,128)}, u32[]{:S(2)}) copy-start(f32[8,512,1024]{2,1,0:T(8,128)} %get-tuple-element.305) | copy-start | bytes 50331652 | tf_op jit(solution)/shard_map/cond/branch_1_fun/while
  270.5 13.3 %copy-start.1 = (f32[8,512,1024]{2,1,0:T(8,128)S(1)}, f32[8,512,1024]{2,1,0:T(8,128)}, u32[]{:S(2)}) copy-start(f32[8,512,1024]{2,1,0:T(8,128)} %get-tuple-element.305) | copy-start | bytes 50331652 | tf_op jit(solution)/shard_map/cond/branch_1_fun/while
  303.9 13.3 %copy-start.1 = (f32[8,512,1024]{2,1,0:T(8,128)S(1)}, f32[8,512,1024]{2,1,0:T(8,128)}, u32[]{:S(2)}) copy-start(f32[8,512,1024]{2,1,0:T(8,128)} %get-tuple-element.305) | copy-start | bytes 50331652 | tf_op jit(solution)/shard_map/cond/branch_1_fun/while
  337.3 13.3 %copy-start.1 = (f32[8,512,1024]{2,1,0:T(8,128)S(1)}, f32[8,512,1024]{2,1,0:T(8,128)}, u32[]{:S(2)}) copy-start(f32[8,512,1024]{2,1,0:T(8,128)} %get-tuple-element.305) | copy-start | bytes 50331652 | tf_op jit(solution)/shard_map/cond/branch_1_fun/while
  370.7 13.3 %copy-start.1 = (f32[8,512,1024]{2,1,0:T(8,128)S(1)}, f32[8,512,1024]{2,1,0:T(8,128)}, u32[]{:S(2)}) copy-start(f32[8,512,1024]{2,1,0:T(8,128)} %get-tuple-element.305) | copy-start | bytes 50331652 | tf_op jit(solution)/shard_map/cond/branch_1_fun/while
  404.1 13.3 %copy-start.1 = (f32[8,512,1024]{2,1,0:T(8,128)S(1)}, f32[8,512,1024]{2,1,0:T(8,128)}, u32[]{:S(2)}) copy-start(f32[8,512,1024]{2,1,0:T(8,128)} %get-tuple-element.305) | copy-start | bytes 50331652 | tf_op jit(solution)/shard_map/cond/branch_1_fun/while
  437.5 13.3 %copy-start.1 = (f32[8,512,1024]{2,1,0:T(8,128)S(1)}, f32[8,512,1024]{2,1,0:T(8,128)}, u32[]{:S(2)}) copy-start(f32[8,512,1024]{2,1,0:T(8,128)} %get-tuple-element.305) | copy-start | bytes 50331652 | tf_op jit(solution)/shard_map/cond/branch_1_fun/while
  462.4 8.9 %copy-start.2 = (s32[4]{0:T(128)S(1)}, s32[4]{0:T(128)}, u32[]{:S(2)}) copy-start(s32[4]{0:T(128)} %param.12) | copy-start | bytes 52
  466.7 53.4 %all-to-all-start.3 = ((bf16[4,256,1024]{2,1,0:T(8,128)(2,1)}), bf16[4,256,1024]{2,1,0:T(8,128)(2,1)}, u32[]{:S(2)}, u32[]{:S(2)}) async-start(bf16[4,256,1024]{2,1,0:T(8,128)(2,1)} %copy.42), calls=%async_computation.3 | async-start | bytes 4194304 | tf_op jit(solution)/shard_map/all_to_all | solution.py:68
Sparse Core Ops, SparseCore 0:
  67.8 57.4 all-gather.2
  126.9 58.2 all-gather.4
where the time goes:
time: 536 us; the launch traced here: 534 us
  matrix products  171 us (32%)
  blocking collectives  105 us (20%)
  waiting for transfers between devices  99.6 us (19%)
  local copies, waits for them, and re-layouts  84 us (16%)
  other arithmetic  51.5 us (10%)
  between operations  13.5 us (3%)
  starting transfers between devices  8.25 us (2%)
    dot_general x8, matrix products, one_block(): jnp.einsum('hqk,khd->qhd', expo.astype(jnp.bfloat16), value_block, prefer...  95.3 us
    dot_general x8, matrix products, one_block(): jnp.einsum('qhd,khd->hqk', query_three, key_block, preferred_element_type...  74.9 us
    all_to_all x1, blocking collectives, local(): lax.all_to_all(k_in[0], 'seq', split_axis=1, concat_axis=0, tiled=True)  54.5 us
    all_to_all x1, blocking collectives, local(): lax.all_to_all(v_in[0], 'seq', split_axis=1, concat_axis=0, tiled=True)  51 us
    all_to_all x1, waiting for transfers between devices, local(): lax.all_to_all(q_in[0], 'seq', split_axis=1, concat_axis=0, tiled=True)  47.3 us
    all_to_all x1, waiting for transfers between devices, local(): lax.all_to_all(attn, 'seq', split_axis=0, concat_axis=1, tiled=True)  47.3 us
    reduce_sum x8, other arithmetic, one_block(): total = total * shrink + jnp.sum(expo, axis=-1)  37 us
    dynamic_slice x16, local copies, waits for them, and re-layouts, one_block(): lax.dynamic_slice_in_dim(value_piece, offset, block, 0)  25.8 us
  transfers between devices with their start and end apart: 4, of which 3 were waited for; matrix products, arithmetic and copies ran while one was open for 2% of the time, Pallas kernels for 0%

commit v1 on v0

--- a/solution.py
+++ b/solution.py
@@ -6,6 +6,29 @@
 
 HD = 128
 masked_score = -1e30
+
+
+def cut_along(value, dim, count):
+    before, after = (value.shape[:dim], value.shape[dim + 1 :])
+    return jnp.moveaxis(value.reshape(*before, count, -1, *after), dim, 0)
+
+
+def in_order(tiles, dim):
+    shape = list(tiles.shape[1:])
+    shape[dim] *= tiles.shape[0]
+    return jnp.moveaxis(tiles, 0, dim).reshape(shape)
+
+
+def sent_to_each(value, axis, split_dim, concat_dim):
+    size, index = (lax.axis_size(axis), lax.axis_index(axis))
+    pieces = cut_along(value, split_dim, size)
+    out = pieces
+    for step in range(1, size):
+        target, source = ((index + step) % size, (index - step) % size)
+        sent = lax.dynamic_index_in_dim(pieces, target, 0)
+        partner_block = lax.ppermute(sent, axis, [(i, (i + step) % size) for i in range(size)])
+        out = lax.dynamic_update_slice_in_dim(out, partner_block, source, axis=0)
+    return in_order(out, concat_dim)
 
 
 def local(q_in, k_in, v_in, timesteps, gate_table):
@@ -65,7 +88,7 @@
 
     top, total, accum = lax.cond(jnp.int32(0) < limit, run_blocks, keep_state, init)
     attn = (accum / total.T[:, :, None]).reshape(length, columns).astype(jnp.bfloat16)
-    token_rows = lax.all_to_all(attn, "seq", split_axis=0, concat_axis=1, tiled=True)
+    token_rows = sent_to_each(attn, "seq", 0, 1)
     steps_count = gate_table.shape[0]
     span_step = lax.dynamic_index_in_dim(timesteps, span_id, 0, keepdims=False)
     picked = (jnp.arange(steps_count) == span_step).astype(jnp.float32)

time: 536 us -> 566 us (1.056); the launches traced: 534 us -> 555 us
  other arithmetic: 51.5 us -> 84.2 us
  matrix products: 171 us -> 186 us
  local copies, waits for them, and re-layouts: 84 us -> 69.9 us
  waiting for transfers between devices: 99.6 us -> 88.2 us
    all_to_all x1 -> x0, waiting for transfers between devices: 47.3 us -> none  [local(): lax.all_to_all(attn, 'seq', split_axis=0, concat_axis=1, tiled=True)]
    ppermute x0 -> x3, waiting for transfers between devices: none -> 35.9 us  [sent_to_each(): lax.ppermute(sent, axis, [(i, (i + step) % size) for i in range(size)])]
    reduce_sum x8, other arithmetic: 37 us -> 65.9 us  [one_block(): total = total * shrink + jnp.sum(expo, axis=-1)]
    dot_general x8, matrix products: 74.9 us -> 91.7 us  [one_block(): jnp.einsum('qhd,khd->hqk', query_three, key_block, preferred_element_type...]
    while x24 -> x8, local copies, waits for them, and re-layouts: 9.48 us -> 0.03 us
    dynamic_slice x16, local copies, waits for them, and re-layouts: 25.8 us -> 18 us  [one_block(): lax.dynamic_slice_in_dim(value_piece, offset, block, 0)]
  transfers between devices with their start and end apart: 4 -> 6, of which waited for: 3 -> 4; matrix products, arithmetic and copies ran while one was open for 2% -> 2% of each run, Pallas kernels for 0% -> 0%
where the time goes in v1:
time: 566 us; the launch traced here: 555 us
  matrix products  186 us (33%)
  blocking collectives  105 us (19%)
  waiting for transfers between devices  88.2 us (16%)
  other arithmetic  84.2 us (15%)
  local copies, waits for them, and re-layouts  69.9 us (12%)
  between operations  13.5 us (2%)
  starting transfers between devices  7.2 us (1%)
    dot_general x8, matrix products, one_block(): jnp.einsum('hqk,khd->qhd', expo.astype(jnp.bfloat16), value_block, prefer...  93.6 us
    dot_general x8, matrix products, one_block(): jnp.einsum('qhd,khd->hqk', query_three, key_block, preferred_element_type...  91.7 us
    reduce_sum x8, other arithmetic, one_block(): total = total * shrink + jnp.sum(expo, axis=-1)  65.9 us
    all_to_all x1, blocking collectives, local(): lax.all_to_all(k_in[0], 'seq', split_axis=1, concat_axis=0, tiled=True)  54.5 us
    all_to_all x1, blocking collectives, local(): lax.all_to_all(v_in[0], 'seq', split_axis=1, concat_axis=0, tiled=True)  51 us
    all_to_all x1, waiting for transfers between devices, local(): lax.all_to_all(q_in[0], 'seq', split_axis=1, concat_axis=0, tiled=True)  47.3 us
    ppermute x3, waiting for transfers between devices, sent_to_each(): lax.ppermute(sent, axis, [(i, (i + step) % size) for i in range(size)])  35.9 us
    dynamic_slice x16, local copies, waits for them, and re-layouts, one_block(): lax.dynamic_slice_in_dim(value_piece, offset, block, 0)  18 us
  transfers between devices with their start and end apart: 6, of which 4 were waited for; matrix products, arithmetic and copies ran while one was open for 2% of the time, Pallas kernels for 0%

profile of v1, /device:TPU:0, one launch (start us, length us, event | category | flops | bytes accessed | tf_op | source)
XLA Modules:
  0.0 555.0 jit_solution(18159525951053642551)
XLA Ops:
  6.5 4.1 copy.54
  10.7 54.5 %all_to_all.54 = bf16[256,4,1024]{0,2,1:T(8,128)(2,1)S(1)} all-to-all(bf16[256,4,1024]{0,2,1:T(8,128)(2,1)} %bitcast.78), channel_id=1, replica_groups=mesh['parts'=2,'span'=4,'seq'=4] {'seq'}, dimensions={1} | all-to-all | bytes 4194304 | tf_op jit(solution)/shard_map/all_to_all | solution.py:37
  65.2 2.5 copy.55
  67.7 4.1 copy.56
  71.8 51.0 %all_to_all.55 = bf16[256,4,1024]{0,2,1:T(8,128)(2,1)S(1)} all-to-all(bf16[256,4,1024]{0,2,1:T(8,128)(2,1)} %bitcast.79), channel_id=1, replica_groups=mesh['parts'=2,'span'=4,'seq'=4] {'seq'}, dimensions={1} | all-to-all | bytes 4194304 | tf_op jit(solution)/shard_map/all_to_all | solution.py:38
  122.8 2.4 copy.57
  125.2 4.1 copy.53
  129.3 3.6 all-to-all-start
  132.9 47.3 %all-to-all-done = bf16[256,4,1024]{0,2,1:T(8,128)(2,1)S(1)} async-done(((bf16[256,4,1024]{0,2,1:T(8,128)(2,1)}), bf16[256,4,1024]{0,2,1:T(8,128)(2,1)S(1)}, u32[]{:S(2)}, u32[]{:S(2)}) %all-to-all-start) | async-done | bytes 2097184 | tf_op jit(solution)/shard_map/all_to_all | solution.py:36
  180.2 5.0 all-gather.5.cloned.1.call-done
  185.2 297.0 %conditional.1 = (f32[8,1024]{1,0:T(8,128)}, f32[1024,8,128]{0,2,1:T(8,128)}) conditional(s32[]{:T(128)} %convert_element_type.44, () %tuple.27, (bf16[4,256,1024]{1,2,0:T(8,128)(2,1)S(1)}, s32[]{:T(128)}, bf16[4096,1024]{1,0:T(8,128)(2,1)}, bf16[4096,1024]{1,0:T(8,128)(2,1)}) %tuple.69), branch_computations={%region_0.0_spmd, %region_1.6_spmd} | conditional | flops 2205205504 | bytes 84412728 | solution.py:89
  185.2 2.4 copy.58
  187.6 2.2 copy.69
  189.8 1.7 copy.52
  191.5 290.8 %while.17 = (s32[]{:T(128)}, f32[8,1024]{1,0:T(8,128)S(1)}, f32[8,1024]{1,0:T(8,128)}, f32[1024,8,128]{0,2,1:T(8,128)}, s32[]{:T(128)}, /*index=5*/bf16[4096,102...) while((s32[]{:T(128)}, f32[8,1024]{1,0:T(8,128)S(1)}, ...), condition=%wide.region_5.5_spmd.clone, body=%wide.region_2.4_spmd.clone.sunk | while | flops 2205205504 | bytes 71829696 | solution.py:84
  191.5 1.7 constant_dynamic-slice_fusion.6
  194.5 11.5 %bitcast_reduce_fusion.2 = (f32[8,1024]{1,0:T(8,128)S(1)}, f32[8,512,1024]{2,1,0:T(8,128)}) fusion(pred[512]{0:T(512)(128)(4,1)S(1)} %add_compare_fusion.2, bf16[512,8,128]{0,2,1:T(8,128)(2,1)} %bitcast.71, bf16[1024,8,128]{2,0,1:T(8,128)(2,1)} %get-tuple-element.353), kind=kOutput, calls=%fused_computation.1.clone.1 | convolution fusion | flops 1086316544 | bytes 19956224 | tf_op jit(solution)/shard_map/cond/branch_1_fun/while/body/eval_jaxpr/qhd,khd->hqk/dot_general | solution.py:65
  206.0 8.2 %fusion.37 = f32[8,1024]{1,0:T(8,128)S(1)} fusion(f32[8,512,1024]{2,1,0:T(8,128)} %get-tuple-element.320, f32[8,1024]{1,0:T(8,128)S(1)} %get-tuple-element.348, pred[512]{0:T(512)(128)(4,1)S(1)} %add_compare_fusion.2), kind=kLoop, calls=%fused_computation.6.clone.1 | loop fusion | flops 20963328 | bytes 16843264 | tf_op jit(solution)/shard_map/cond/branch_1_fun/while/body/eval_jaxpr/reduce_sum | solution.py:73
  215.5 10.7 %bitcast_add_fusion.2 = f32[1024,8,128]{0,2,1:T(8,128)} fusion(f32[1024,8,128]{0,2,1:T(8,128)} %get-tuple-element.338, bf16[512,8,128]{0,2,1:T(8,128)(2,1)S(1)} %bitcast.72, f32[8,512,1024]{2,1,0:T(8,128)} %get-tuple-element.320, f32[8,1024]{1,0:T(8,128)S(1)} %get-tuple-element.348, pred[512]{0:T(512)(128)(4,1)S(1)} %add_compare_fusion.2, ...), kind=kOutput, calls=%fused_computation.10.clone.1 | convolution fusion | flops 1097859072 | bytes 26280448 | tf_op jit(solution)/shard_map/cond/branch_1_fun/while/body/eval_jaxpr/hqk,khd->qhd/dot_general | solution.py:74
  226.1 1.7 constant_dynamic-slice_fusion.6
  229.2 11.5 %bitcast_reduce_fusion.2 = (f32[8,1024]{1,0:T(8,128)S(1)}, f32[8,512,1024]{2,1,0:T(8,128)}) fusion(pred[512]{0:T(512)(128)(4,1)S(1)} %add_compare_fusion.2, bf16[512,8,128]{0,2,1:T(8,128)(2,1)} %bitcast.71, bf16[1024,8,128]{2,0,1:T(8,128)(2,1)} %get-tuple-element.353), kind=kOutput, calls=%fused_computation.1.clone.1 | convolution fusion | flops 1086316544 | bytes 19956224 | tf_op jit(solution)/shard_map/cond/branch_1_fun/while/body/eval_jaxpr/qhd,khd->hqk/dot_general | solution.py:65
  240.7 8.2 %fusion.37 = f32[8,1024]{1,0:T(8,128)S(1)} fusion(f32[8,512,1024]{2,1,0:T(8,128)} %get-tuple-element.320, f32[8,1024]{1,0:T(8,128)S(1)} %get-tuple-element.348, pred[512]{0:T(512)(128)(4,1)S(1)} %add_compare_fusion.2), kind=kLoop, calls=%fused_computation.6.clone.1 | loop fusion | flops 20963328 | bytes 16843264 | tf_op jit(solution)/shard_map/cond/branch_1_fun/while/body/eval_jaxpr/reduce_sum | solution.py:73
  248.9 1.4 fusion.38
  250.9 11.8 %bitcast_add_fusion.2 = f32[1024,8,128]{0,2,1:T(8,128)} fusion(f32[1024,8,128]{0,2,1:T(8,128)} %get-tuple-element.338, bf16[512,8,128]{0,2,1:T(8,128)(2,1)S(1)} %bitcast.72, f32[8,512,1024]{2,1,0:T(8,128)} %get-tuple-element.320, f32[8,1024]{1,0:T(8,128)S(1)} %get-tuple-element.348, pred[512]{0:T(512)(128)(4,1)S(1)} %add_compare_fusion.2, ...), kind=kOutput, calls=%fused_computation.10.clone.1 | convolution fusion | flops 1097859072 | bytes 26280448 | tf_op jit(solution)/shard_map/cond/branch_1_fun/while/body/eval_jaxpr/hqk,khd->qhd/dot_general | solution.py:74
  262.7 1.7 constant_dynamic-slice_fusion.6
  265.8 11.5 %bitcast_reduce_fusion.2 = (f32[8,1024]{1,0:T(8,128)S(1)}, f32[8,512,1024]{2,1,0:T(8,128)}) fusion(pred[512]{0:T(512)(128)(4,1)S(1)} %add_compare_fusion.2, bf16[512,8,128]{0,2,1:T(8,128)(2,1)} %bitcast.71, bf16[1024,8,128]{2,0,1:T(8,128)(2,1)} %get-tuple-element.353), kind=kOutput, calls=%fused_computation.1.clone.1 | convolution fusion | flops 1086316544 | bytes 19956224 | tf_op jit(solution)/shard_map/cond/branch_1_fun/while/body/eval_jaxpr/qhd,khd->hqk/dot_general | solution.py:65
  277.3 8.2 %fusion.37 = f32[8,1024]{1,0:T(8,128)S(1)} fusion(f32[8,512,1024]{2,1,0:T(8,128)} %get-tuple-element.320, f32[8,1024]{1,0:T(8,128)S(1)} %get-tuple-element.348, pred[512]{0:T(512)(128)(4,1)S(1)} %add_compare_fusion.2), kind=kLoop, calls=%fused_computation.6.clone.1 | loop fusion | flops 20963328 | bytes 16843264 | tf_op jit(solution)/shard_map/cond/branch_1_fun/while/body/eval_jaxpr/reduce_sum | solution.py:73
  285.5 1.4 fusion.38
  287.4 11.8 %bitcast_add_fusion.2 = f32[1024,8,128]{0,2,1:T(8,128)} fusion(f32[1024,8,128]{0,2,1:T(8,128)} %get-tuple-element.338, bf16[512,8,128]{0,2,1:T(8,128)(2,1)S(1)} %bitcast.72, f32[8,512,1024]{2,1,0:T(8,128)} %get-tuple-element.320, f32[8,1024]{1,0:T(8,128)S(1)} %get-tuple-element.348, pred[512]{0:T(512)(128)(4,1)S(1)} %add_compare_fusion.2, ...), kind=kOutput, calls=%fused_computation.10.clone.1 | convolution fusion | flops 1097859072 | bytes 26280448 | tf_op jit(solution)/shard_map/cond/branch_1_fun/while/body/eval_jaxpr/hqk,khd->qhd/dot_general | solution.py:74
  299.3 1.7 constant_dynamic-slice_fusion.6
  302.4 11.5 %bitcast_reduce_fusion.2 = (f32[8,1024]{1,0:T(8,128)S(1)}, f32[8,512,1024]{2,1,0:T(8,128)}) fusion(pred[512]{0:T(512)(128)(4,1)S(1)} %add_compare_fusion.2, bf16[512,8,128]{0,2,1:T(8,128)(2,1)} %bitcast.71, bf16[1024,8,128]{2,0,1:T(8,128)(2,1)} %get-tuple-element.353), kind=kOutput, calls=%fused_computation.1.clone.1 | convolution fusion | flops 1086316544 | bytes 19956224 | tf_op jit(solution)/shard_map/cond/branch_1_fun/while/body/eval_jaxpr/qhd,khd->hqk/dot_general | solution.py:65
  313.9 8.2 %fusion.37 = f32[8,1024]{1,0:T(8,128)S(1)} fusion(f32[8,512,1024]{2,1,0:T(8,128)} %get-tuple-element.320, f32[8,1024]{1,0:T(8,128)S(1)} %get-tuple-element.348, pred[512]{0:T(512)(128)(4,1)S(1)} %add_compare_fusion.2), kind=kLoop, calls=%fused_computation.6.clone.1 | loop fusion | flops 20963328 | bytes 16843264 | tf_op jit(solution)/shard_map/cond/branch_1_fun/while/body/eval_jaxpr/reduce_sum | solution.py:73
  322.1 1.4 fusion.38
  324.0 11.8 %bitcast_add_fusion.2 = f32[1024,8,128]{0,2,1:T(8,128)} fusion(f32[1024,8,128]{0,2,1:T(8,128)} %get-tuple-element.338, bf16[512,8,128]{0,2,1:T(8,128)(2,1)S(1)} %bitcast.72, f32[8,512,1024]{2,1,0:T(8,128)} %get-tuple-element.320, f32[8,1024]{1,0:T(8,128)S(1)} %get-tuple-element.348, pred[512]{0:T(512)(128)(4,1)S(1)} %add_compare_fusion.2, ...), kind=kOutput, calls=%fused_computation.10.clone.1 | convolution fusion | flops 1097859072 | bytes 26280448 | tf_op jit(solution)/shard_map/cond/branch_1_fun/while/body/eval_jaxpr/hqk,khd->qhd/dot_general | solution.py:74
  335.9 1.7 constant_dynamic-slice_fusion.6
  339.0 11.5 %bitcast_reduce_fusion.2 = (f32[8,1024]{1,0:T(8,128)S(1)}, f32[8,512,1024]{2,1,0:T(8,128)}) fusion(pred[512]{0:T(512)(128)(4,1)S(1)} %add_compare_fusion.2, bf16[512,8,128]{0,2,1:T(8,128)(2,1)} %bitcast.71, bf16[1024,8,128]{2,0,1:T(8,128)(2,1)} %get-tuple-element.353), kind=kOutput, calls=%fused_computation.1.clone.1 | convolution fusion | flops 1086316544 | bytes 19956224 | tf_op jit(solution)/shard_map/cond/branch_1_fun/while/body/eval_jaxpr/qhd,khd->hqk/dot_general | solution.py:65
  350.4 8.2 %fusion.37 = f32[8,1024]{1,0:T(8,128)S(1)} fusion(f32[8,512,1024]{2,1,0:T(8,128)} %get-tuple-element.320, f32[8,1024]{1,0:T(8,128)S(1)} %get-tuple-element.348, pred[512]{0:T(512)(128)(4,1)S(1)} %add_compare_fusion.2), kind=kLoop, calls=%fused_computation.6.clone.1 | loop fusion | flops 20963328 | bytes 16843264 | tf_op jit(solution)/shard_map/cond/branch_1_fun/while/body/eval_jaxpr/reduce_sum | solution.py:73
  358.7 1.4 fusion.38
  360.6 11.8 %bitcast_add_fusion.2 = f32[1024,8,128]{0,2,1:T(8,128)} fusion(f32[1024,8,128]{0,2,1:T(8,128)} %get-tuple-element.338, bf16[512,8,128]{0,2,1:T(8,128)(2,1)S(1)} %bitcast.72, f32[8,512,1024]{2,1,0:T(8,128)} %get-tuple-element.320, f32[8,1024]{1,0:T(8,128)S(1)} %get-tuple-element.348, pred[512]{0:T(512)(128)(4,1)S(1)} %add_compare_fusion.2, ...), kind=kOutput, calls=%fused_computation.10.clone.1 | convolution fusion | flops 1097859072 | bytes 26280448 | tf_op jit(solution)/shard_map/cond/branch_1_fun/while/body/eval_jaxpr/hqk,khd->qhd/dot_general | solution.py:74
  372.5 1.7 constant_dynamic-slice_fusion.6
  375.5 11.5 %bitcast_reduce_fusion.2 = (f32[8,1024]{1,0:T(8,128)S(1)}, f32[8,512,1024]{2,1,0:T(8,128)}) fusion(pred[512]{0:T(512)(128)(4,1)S(1)} %add_compare_fusion.2, bf16[512,8,128]{0,2,1:T(8,128)(2,1)} %bitcast.71, bf16[1024,8,128]{2,0,1:T(8,128)(2,1)} %get-tuple-element.353), kind=kOutput, calls=%fused_computation.1.clone.1 | convolution fusion | flops 1086316544 | bytes 19956224 | tf_op jit(solution)/shard_map/cond/branch_1_fun/while/body/eval_jaxpr/qhd,khd->hqk/dot_general | solution.py:65
  387.0 8.2 %fusion.37 = f32[8,1024]{1,0:T(8,128)S(1)} fusion(f32[8,512,1024]{2,1,0:T(8,128)} %get-tuple-element.320, f32[8,1024]{1,0:T(8,128)S(1)} %get-tuple-element.348, pred[512]{0:T(512)(128)(4,1)S(1)} %add_compare_fusion.2), kind=kLoop, calls=%fused_computation.6.clone.1 | loop fusion | flops 20963328 | bytes 16843264 | tf_op jit(solution)/shard_map/cond/branch_1_fun/while/body/eval_jaxpr/reduce_sum | solution.py:73
  395.3 1.4 fusion.38
  397.2 11.8 %bitcast_add_fusion.2 = f32[1024,8,128]{0,2,1:T(8,128)} fusion(f32[1024,8,128]{0,2,1:T(8,128)} %get-tuple-element.338, bf16[512,8,128]{0,2,1:T(8,128)(2,1)S(1)} %bitcast.72, f32[8,512,1024]{2,1,0:T(8,128)} %get-tuple-element.320, f32[8,1024]{1,0:T(8,128)S(1)} %get-tuple-element.348, pred[512]{0:T(512)(128)(4,1)S(1)} %add_compare_fusion.2, ...), kind=kOutput, calls=%fused_computation.10.clone.1 | convolution fusion | flops 1097859072 | bytes 26280448 | tf_op jit(solution)/shard_map/cond/branch_1_fun/while/body/eval_jaxpr/hqk,khd->qhd/dot_general | solution.py:74
  409.1 1.7 constant_dynamic-slice_fusion.6
  412.1 11.5 %bitcast_reduce_fusion.2 = (f32[8,1024]{1,0:T(8,128)S(1)}, f32[8,512,1024]{2,1,0:T(8,128)}) fusion(pred[512]{0:T(512)(128)(4,1)S(1)} %add_compare_fusion.2, bf16[512,8,128]{0,2,1:T(8,128)(2,1)} %bitcast.71, bf16[1024,8,128]{2,0,1:T(8,128)(2,1)} %get-tuple-element.353), kind=kOutput, calls=%fused_computation.1.clone.1 | convolution fusion | flops 1086316544 | bytes 19956224 | tf_op jit(solution)/shard_map/cond/branch_1_fun/while/body/eval_jaxpr/qhd,khd->hqk/dot_general | solution.py:65
  423.6 8.2 %fusion.37 = f32[8,1024]{1,0:T(8,128)S(1)} fusion(f32[8,512,1024]{2,1,0:T(8,128)} %get-tuple-element.320, f32[8,1024]{1,0:T(8,128)S(1)} %get-tuple-element.348, pred[512]{0:T(512)(128)(4,1)S(1)} %add_compare_fusion.2), kind=kLoop, calls=%fused_computation.6.clone.1 | loop fusion | flops 20963328 | bytes 16843264 | tf_op jit(solution)/shard_map/cond/branch_1_fun/while/body/eval_jaxpr/reduce_sum | solution.py:73
  433.8 11.8 %bitcast_add_fusion.2 = f32[1024,8,128]{0,2,1:T(8,128)} fusion(f32[1024,8,128]{0,2,1:T(8,128)} %get-tuple-element.338, bf16[512,8,128]{0,2,1:T(8,128)(2,1)S(1)} %bitcast.72, f32[8,512,1024]{2,1,0:T(8,128)} %get-tuple-element.320, f32[8,1024]{1,0:T(8,128)S(1)} %get-tuple-element.348, pred[512]{0:T(512)(128)(4,1)S(1)} %add_compare_fusion.2, ...), kind=kOutput, calls=%fused_computation.10.clone.1 | convolution fusion | flops 1097859072 | bytes 26280448 | tf_op jit(solution)/shard_map/cond/branch_1_fun/while/body/eval_jaxpr/hqk,khd->qhd/dot_general | solution.py:74
  445.7 1.7 constant_dynamic-slice_fusion.6
  448.7 11.5 %bitcast_reduce_fusion.2 = (f32[8,1024]{1,0:T(8,128)S(1)}, f32[8,512,1024]{2,1,0:T(8,128)}) fusion(pred[512]{0:T(512)(128)(4,1)S(1)} %add_compare_fusion.2, bf16[512,8,128]{0,2,1:T(8,128)(2,1)} %bitcast.71, bf16[1024,8,128]{2,0,1:T(8,128)(2,1)} %get-tuple-element.353), kind=kOutput, calls=%fused_computation.1.clone.1 | convolution fusion | flops 1086316544 | bytes 19956224 | tf_op jit(solution)/shard_map/cond/branch_1_fun/while/body/eval_jaxpr/qhd,khd->hqk/dot_general | solution.py:65
  460.2 8.2 %fusion.37 = f32[8,1024]{1,0:T(8,128)S(1)} fusion(f32[8,512,1024]{2,1,0:T(8,128)} %get-tuple-element.320, f32[8,1024]{1,0:T(8,128)S(1)} %get-tuple-element.348, pred[512]{0:T(512)(128)(4,1)S(1)} %add_compare_fusion.2), kind=kLoop, calls=%fused_computation.6.clone.1 | loop fusion | flops 20963328 | bytes 16843264 | tf_op jit(solution)/shard_map/cond/branch_1_fun/while/body/eval_jaxpr/reduce_sum | solution.py:73
  468.5 1.4 fusion.38
  470.4 11.8 %bitcast_add_fusion.2 = f32[1024,8,128]{0,2,1:T(8,128)} fusion(f32[1024,8,128]{0,2,1:T(8,128)} %get-tuple-element.338, bf16[512,8,128]{0,2,1:T(8,128)(2,1)S(1)} %bitcast.72, f32[8,512,1024]{2,1,0:T(8,128)} %get-tuple-element.320, f32[8,1024]{1,0:T(8,128)S(1)} %get-tuple-element.348, pred[512]{0:T(512)(128)(4,1)S(1)} %add_compare_fusion.2, ...), kind=kOutput, calls=%fused_computation.10.clone.1 | convolution fusion | flops 1097859072 | bytes 26280448 | tf_op jit(solution)/shard_map/cond/branch_1_fun/while/body/eval_jaxpr/hqk,khd->qhd/dot_general | solution.py:74
  482.2 2.8 divide_convert_fusion
  485.0 2.8 reshape.89
  487.8 3.0 copy.66
  491.6 1.5 collective-permute-start
  493.1 14.6 %collective-permute-done = bf16[1,256,1024]{2,1,0:T(8,128)(2,1)S(1)} collective-permute-done((bf16[1,256,1024]{2,1,0:T(8,128)(2,1)}, bf16[1,256,1024]{2,1,0:T(8,128)(2,1)S(1)}, u32[]{:S(2)}, u32[]{:S(2)}) %collective-permute-start) | collective-permute-done | bytes 524320 | tf_op jit(solution)/shard_map/ppermute | solution.py:29
  509.4 1.4 collective-permute-start.2
  512.5 21.3 %collective-permute-done.1 = bf16[1,256,1024]{2,1,0:T(8,128)(2,1)} collective-permute-done((bf16[1,256,1024]{2,1,0:T(8,128)(2,1)}, bf16[1,256,1024]{2,1,0:T(8,128)(2,1)}, u32[]{:S(2)}, u32[]{:S(2)}) %collective-permute-start.1) | collective-permute-done | bytes 524320 | tf_op jit(solution)/shard_map/ppermute | solution.py:29
  534.9 2.4 convert_bitcast_fusion
  537.4 5.4 copy.62
  542.8 2.6 fusion.15
  545.3 2.9 copy.63
  (62 shorter events, 22.7 us)
Async XLA Ops:
  6.5 505.0 %copy-start = (f32[32,4096]{1,0:T(8,128)S(1)}, f32[32,4096]{1,0:T(8,128)}, u32[]{:S(2)}) copy-start(f32[32,4096]{1,0:T(8,128)} %param.13) | copy-start | bytes 1572868
  6.5 173.7 %all-gather.3.cloned.1.call-start = ((), (), s32[]{:S(2)}) async-start(), calls=%async_computation.3 | async-start | bytes 10485760 | tf_op jit(solution)/shard_map/all_gather | solution.py:52
  67.7 117.5 %all-gather.5.cloned.1.call-start = ((), (), s32[]{:S(2)}) async-start(), calls=%async_computation.4 | async-start | bytes 10485760 | tf_op jit(solution)/shard_map/all_gather | solution.py:53
  129.3 50.9 %all-to-all-start = ((bf16[256,4,1024]{0,2,1:T(8,128)(2,1)}), bf16[256,4,1024]{0,2,1:T(8,128)(2,1)S(1)}, u32[]{:S(2)}, u32[]{:S(2)}) async-start(bf16[256,4,1024]{0,2,1:T(8,128)(2,1)} %bitcast.76), calls=%async_computation | async-start | bytes 4194304 | tf_op jit(solution)/shard_map/all_to_all | solution.py:36
  487.8 23.1 %copy-start.1 = (s32[4]{0:T(128)S(1)}, s32[4]{0:T(128)}, u32[]{:S(2)}) copy-start(s32[4]{0:T(128)} %param.12) | copy-start | bytes 52
  491.6 16.1 %collective-permute-start = (bf16[1,256,1024]{2,1,0:T(8,128)(2,1)}, bf16[1,256,1024]{2,1,0:T(8,128)(2,1)S(1)}, u32[]{:S(2)}, u32[]{:S(2)}) collective-permute-start(bf16[1,256,1024]{2,1,0:T(8,128)(2,1)} %constant_dynamic-slice_fusion.4), channel_id=1, source_target_pairs={{0,1},{1,2},{2,3},{3,0},{4,5},{5,6},{6,7},{7,4},{8,9},{9,10},{10,1... | collective-permute-start | bytes 1572872 | tf_op jit(solution)/shard_map/ppermute | solution.py:29
  508.8 25.0 %collective-permute-start.1 = (bf16[1,256,1024]{2,1,0:T(8,128)(2,1)}, bf16[1,256,1024]{2,1,0:T(8,128)(2,1)}, u32[]{:S(2)}, u32[]{:S(2)}) collective-permute-start(bf16[1,256,1024]{2,1,0:T(8,128)(2,1)} %get-tuple-element.260), channel_id=1, source_target_pairs={{0,2},{1,3},{2,0},{3,1},{4,6},{5,7},{6,4},{7,5},{8,10},{9,11},{10,... | collective-permute-start | bytes 1572872 | tf_op jit(solution)/shard_map/ppermute | solution.py:29
  509.4 25.5 %collective-permute-start.2 = (bf16[1,256,1024]{2,1,0:T(8,128)(2,1)}, bf16[1,256,1024]{2,1,0:T(8,128)(2,1)S(1)}, u32[]{:S(2)}, u32[]{:S(2)}) collective-permute-start(bf16[1,256,1024]{2,1,0:T(8,128)(2,1)} %get-tuple-element.259), channel_id=1, source_target_pairs={{0,3},{1,0},{2,1},{3,2},{4,7},{5,4},{6,5},{7,6},{8,11},{9,8},{10,9... | collective-permute-start | bytes 1572872 | tf_op jit(solution)/shard_map/ppermute | solution.py:29
Sparse Core Ops, SparseCore 0:
  67.8 57.4 all-gather.2
  126.9 58.2 all-gather.4
